TPU v7x, 32 devices: a whole 2x2x4 slice. The times are simulated.
32 devices in a mesh: grp: 4 (over x, core), inner: 8 (over z, y).
Axes of the slice: x: 2, y: 2, z: 4, core: 2. Of those that a mesh axis runs over, the one named last changes fastest.
Arguments:
- electric: float32 [3, 16, 128, 512], P(None, None, 'inner', 'grp'), may hold values from -6 to 6
- magnetic: float32 [3, 16, 128, 512], P(None, None, 'inner', 'grp'), may hold values from -6 to 6
- material_ids: int32 [16, 128, 512], P(None, 'inner', 'grp'), may hold values from 0 to 7
- update_ca: float32 [8], replicated, may hold values from 0.6 to 1
- update_cb: float32 [8], replicated, may hold values from 0.12 to 0.45
- face_ranges: int32 [8, 4, 4], P('inner', 'grp'), may hold values from 0 to 128, as said below
- band_table: int32 [32], replicated, may hold values from 0 to 31, each once
Outputs:
- electric_out: float32 [3, 16, 128, 512], P(None, None, 'inner', 'grp')
- magnetic_out: float32 [3, 16, 128, 512], P(None, None, 'inner', 'grp')
- far_field: float32 [32, 8, 128], P(('grp', 'inner'))
Inputs may be any that keep to these rules, and one draw needn't show every extreme that they name: `face_ranges`: one box [x0, x1) x [y0, y1) with x0 <= 32, x1 >= 96, y0 <= 128, y1 >= 384 is clipped to each tile: entries are (clip(x0 - i * 16), clip(x1 - i * 16), clip(y0 - j * 128), clip(y1 - j * 128)), each clip into [0, tile width].
All inputs are finite; a program needn't handle non-finite values.
Results may differ from a plain program's by a relative error of at most 0.0003.
Values sent between devices are 32-bit elements; how exact they have to be, the bound alone decides.
A program may use at most 64 MiB of HBM per device.

v0:
```python
import functools
import math

import jax
import jax.numpy as jnp
import numpy as np
from jax import lax
from jax.experimental import pallas as pl
from jax.experimental.pallas import tpu as pltpu
from jax.sharding import PartitionSpec as P

STEPS = 8
FREQS = 32
ANG_BAND = 4
NMAT = 8
ZF = 8
NZ = 16
CX = 16
CY = 128
PITCH = 24
BASE = 8
MESH = pl.DeviceIdType.MESH


def tables(bands, groups):
    f = np.tile(np.arange(FREQS, dtype=np.int64) + 1, ANG_BAND)
    b = np.repeat(np.arange(ANG_BAND, dtype=np.int64) * 33 // ANG_BAND - 16, FREQS)
    a = np.arange(bands, dtype=np.int64) - bands // 2

    def both(turns, period):
        angle = (turns % period) * (2.0 * math.pi / period)
        return np.cos(angle).astype(np.float32), np.sin(angle).astype(np.float32)

    y = np.arange(CY, dtype=np.int64)[:, None]
    proj = np.concatenate(both(f * b * y, 4096), axis=1)
    time = np.stack(both(f * np.arange(STEPS, dtype=np.int64)[:, None], 128))
    y_start = np.stack(both(f * b * CY * np.arange(groups, dtype=np.int64)[:, None], 4096))
    cell = np.stack(both(f * a[:, None], 4096))
    block = np.stack(both(f * a[:, None] * CX, 4096))
    return proj, time, y_start, cell, block


def kernel(
    ny, nx, scale,
    e_in, h_in, ids, ca, cb, face, bands, proj, time, y_start, cell, block,
    e_out, h_out, far_out,
    ep, hp, coef_a, coef_b,
    xs_r, xs_l, ys_r, ys_l, xr_l, xr_r, yr_l, yr_r, cor_x, cor_y,
    sample, acc, cols, phase, f_send, f_recv,
    send_sem, recv_sem, f_send_sem, f_recv_sem,
):
    iy = lax.axis_index("grp")
    ix = lax.axis_index("inner")
    total = ny * nx
    me = iy * nx + ix
    lane = lax.broadcasted_iota(jnp.int32, (CX, CY), 1)
    row = lax.broadcasted_iota(jnp.int32, (CX, CY), 0)

    for buf in (xr_l, xr_r, yr_l, yr_r, cor_x, cor_y):
        buf[...] = jnp.zeros(buf.shape, jnp.float32)

    barrier = pltpu.get_barrier_semaphore()

    def greet(k, carry):
        other = lax.rem(me + k, total)
        pl.semaphore_signal(
            barrier, inc=1, device_id=(lax.div(other, nx), lax.rem(other, nx)), device_id_type=MESH
        )
        return carry

    lax.fori_loop(1, total, greet, 0)

    def at(z, shift=0):
        return pl.ds(z * PITCH + BASE + shift, CX)

    def plane(x):
        return pl.ds(BASE + x, NZ, stride=PITCH)

    for c in range(3):
        for z in range(NZ):
            ep[c, at(z), :] = e_in[c, pl.ds(z * CX, CX), :]
            hp[c, at(z), :] = h_in[c, pl.ds(z * CX, CX), :]
    for z in range(NZ):
        here = ids[pl.ds(z * CX, CX), :]
        va = jnp.zeros((CX, CY), jnp.float32)
        vb = jnp.zeros((CX, CY), jnp.float32)
        for m in range(NMAT):
            chosen = here == m
            va = jnp.where(chosen, ca[m], va)
            vb = jnp.where(chosen, cb[m], vb)
        coef_a[pl.ds(z * CX, CX), :] = va
        coef_b[pl.ds(z * CX, CX), :] = vb
    sample[...] = jnp.zeros(sample.shape, jnp.float32)
    acc[...] = jnp.zeros(acc.shape, jnp.float32)
    on_face = (row >= face[0]) & (row < face[1]) & (lane >= face[2]) & (lane < face[3])
    inside_x = jnp.where(ix > 0, 1.0, 0.0).astype(jnp.float32)
    inside_y = jnp.where(iy > 0, 1.0, 0.0).astype(jnp.float32)

    def power(bit, carry):
        pr, pi, br, bi = carry
        take = lax.rem(lax.shift_right_logical(ix, bit), 2) == 1
        nr = pr * br - pi * bi
        ni = pr * bi + pi * br
        return (
            jnp.where(take, nr, pr),
            jnp.where(take, ni, pi),
            br * br - bi * bi,
            2.0 * br * bi,
        )

    rows_at_once = 8
    for start in range(0, total, rows_at_once):
        part = pl.ds(start, rows_at_once)
        carry = (
            jnp.full((rows_at_once, CY), scale, jnp.float32),
            jnp.zeros((rows_at_once, CY), jnp.float32),
            block[0, part, :],
            block[1, part, :],
        )
        for bit in range(max(1, (nx - 1).bit_length())):
            carry = power(bit, carry)
        phase[0, part, :] = carry[0]
        phase[1, part, :] = carry[1]

    pl.semaphore_wait(barrier, total - 1)

    has_xr, has_xl = ix < nx - 1, ix > 0
    has_yr, has_yl = iy < ny - 1, iy > 0

    def copies(n):
        return (
            (has_xr, has_xl, xs_r.at[n], xr_l.at[n], (iy, ix + 1)),
            (has_xl, has_xr, xs_l.at[n], xr_r.at[n], (iy, ix - 1)),
            (has_yr, has_yl, ys_r.at[n], yr_l.at[n], (iy + 1, ix)),
            (has_yl, has_yr, ys_l.at[n], yr_r.at[n], (iy - 1, ix)),
            (has_xr & has_yl, has_xl & has_yr, xs_r.at[n, pl.ds(0, NZ)], cor_x.at[n], (iy - 1, ix + 1)),
            (has_xl & has_yr, has_xr & has_yl, ys_r.at[n, pl.ds(0, 8)], cor_y.at[n], (iy + 1, ix - 1)),
        )

    def remote(n, i, src, dst, device):
        return pltpu.make_async_remote_copy(
            src_ref=src,
            dst_ref=dst,
            send_sem=send_sem.at[i],
            recv_sem=recv_sem.at[n, i],
            device_id=device,
            device_id_type=MESH,
        )

    def add_sample(n):
        g = jnp.dot(
            sample[...], proj[...], precision=lax.Precision.HIGHEST, preferred_element_type=jnp.float32
        )
        g_re, g_im = g[:, :CY], g[:, CY:]
        ct = time[0, pl.ds(n, 1), :]
        st = time[1, pl.ds(n, 1), :]
        acc[0] += ct * g_re + st * g_im
        acc[1] += ct * g_im - st * g_re

    def step(n, carry):
        last = jnp.zeros((CX, CY), jnp.float32)
        first = jnp.zeros((CX, CY), jnp.float32)
        for g, (field, c) in enumerate(((ep, 0), (ep, 1), (ep, 2), (hp, 1), (hp, 2))):
            xs_r[n, pl.ds(g * NZ, NZ), :] = field[c, plane(CX - 1), :]
        for g, c in enumerate((1, 2)):
            xs_l[n, pl.ds(g * NZ, NZ), :] = ep[c, plane(0), :]
        for z in range(NZ):
            for g, (field, c) in enumerate(((ep, 0), (ep, 1), (ep, 2), (hp, 0), (hp, 2))):
                spot = g * NZ + z
                last = jnp.where(lane == spot, pltpu.roll(field[c, at(z), :], (spot - CY + 1) % CY, 1), last)
            for g, c in enumerate((0, 2)):
                spot = g * NZ + z
                value = ep[c, at(z), :]
                first = jnp.where(lane == spot, pltpu.roll(value, spot, 1) if spot else value, first)
        ys_r[n] = last
        ys_l[n] = first
        for i, (sends, _, src, dst, device) in enumerate(copies(n)):
            @pl.when(sends)
            def _(i=i, src=src, dst=dst, device=device):
                remote(n, i, src, dst, device).start()

        add_sample(jnp.maximum(n - 1, 0))

        for i, (_, receives, src, dst, _) in enumerate(copies(n)):
            @pl.when(receives)
            def _(i=i, src=src, dst=dst):
                remote(n, i, src, dst, (iy, ix)).wait_recv()

        ex, ey, ez, hy, hz = (xr_l[n, pl.ds(g * NZ, NZ), :] for g in range(5))
        ey0, ez0 = xs_l[n, pl.ds(0, NZ), :], xs_l[n, pl.ds(NZ, NZ), :]
        ep[1, plane(CX), :] = xr_r[n, pl.ds(0, NZ), :]
        ep[2, plane(CX), :] = xr_r[n, pl.ds(NZ, NZ), :]
        ex_z = jnp.where(row == NZ - 1, 0.0, pltpu.roll(ex, NZ - 1, 0))
        ex_y = pltpu.roll(jnp.where(lane == 0, cor_x[n], ex), CY - 1, 1)
        hp[1, plane(-1), :] = inside_x * (hy - 0.5 * ((ex_z - ex) - (ez0 - ez)))
        hp[2, plane(-1), :] = inside_x * (hz - 0.5 * ((ey0 - ey) - (ex_y - ex)))

        packed, own = yr_l[n], ys_l[n]
        ex = packed
        ey, ez, hx, hz = (pltpu.roll(packed, CY - g * NZ, 1) for g in range(1, 5))
        ex0, ez0 = own, pltpu.roll(own, CY - NZ, 1)
        ey_z = jnp.where(lane == NZ - 1, 0.0, pltpu.roll(ey, CY - 1, 1))
        corner = pltpu.roll(cor_y[n], CY - NZ, 1)[0:1, :]
        ey_x = jnp.where(row == CX - 1, corner, pltpu.roll(ey, CX - 1, 0))
        hx_col = inside_y * (hx - 0.5 * ((ez0 - ez) - (ey_z - ey)))
        hz_col = inside_y * (hz - 0.5 * ((ey_x - ey) - (ex0 - ex)))

        after = yr_r[n]
        zero = jnp.zeros((CX, CY), jnp.float32)
        for z in range(NZ):
            ex, ey, ez = (ep[c, at(z), :] for c in range(3))
            ex_z = ep[0, at(z + 1), :] if z < NZ - 1 else zero
            ey_z = ep[1, at(z + 1), :] if z < NZ - 1 else zero
            ey_x = ep[1, at(z, 1), :]
            ez_x = ep[2, at(z, 1), :]
            ex_y = jnp.where(
                lane == CY - 1, pltpu.roll(after, CY - 1 - z, 1), pltpu.roll(ex, CY - 1, 1)
            )
            ez_y = jnp.where(
                lane == CY - 1, pltpu.roll(after, CY - 1 - NZ - z, 1), pltpu.roll(ez, CY - 1, 1)
            )
            hp[0, at(z), :] = hp[0, at(z), :] - 0.5 * ((ez_y - ez) - (ey_z - ey))
            hp[1, at(z), :] = hp[1, at(z), :] - 0.5 * ((ex_z - ex) - (ez_x - ez))
            hp[2, at(z), :] = hp[2, at(z), :] - 0.5 * ((ey_x - ey) - (ex_y - ex))
        for z in range(NZ):
            hx, hy, hz = (hp[c, at(z), :] for c in range(3))
            hx_z = hp[0, at(z - 1), :] if z else zero
            hy_z = hp[1, at(z - 1), :] if z else zero
            hy_x = hp[1, at(z, -1), :]
            hz_x = hp[2, at(z, -1), :]
            hx_y = jnp.where(lane == 0, pltpu.roll(hx_col, CY - z, 1) if z else hx_col, pltpu.roll(hx, 1, 1))
            hz_y = jnp.where(lane == 0, pltpu.roll(hz_col, CY - z, 1) if z else hz_col, pltpu.roll(hz, 1, 1))
            va, vb = coef_a[pl.ds(z * CX, CX), :], coef_b[pl.ds(z * CX, CX), :]
            ex = va * ep[0, at(z), :] + vb * ((hz - hz_y) - (hy - hy_z))
            ey = va * ep[1, at(z), :] + vb * ((hx - hx_z) - (hz - hz_x))
            ep[0, at(z), :] = ex
            ep[1, at(z), :] = ey
            ep[2, at(z), :] = va * ep[2, at(z), :] + vb * ((hy - hy_x) - (hx - hx_y))
            if z == ZF:
                for c, value in enumerate((ex, ey, hx, hy)):
                    sample[pl.ds(c * CX, CX), :] = jnp.where(on_face, value, 0.0)

        for i, (sends, _, src, dst, device) in enumerate(copies(n)):
            @pl.when(sends)
            def _(i=i, src=src, dst=dst, device=device):
                remote(n, i, src, dst, device).wait_send()
        return carry

    lax.fori_loop(0, STEPS, step, 0)
    add_sample(STEPS - 1)

    yr = y_start[0, pl.ds(iy, 1), :]
    yi = y_start[1, pl.ds(iy, 1), :]
    col_re = acc[0] * yr - acc[1] * yi
    acc[1] = acc[0] * yi + acc[1] * yr
    acc[0] = col_re
    for part in range(2):
        for x in range(CX):
            four = acc[part, pl.ds(x, 4, stride=CX), :]
            cols[part, x, pl.ds(0, 4), :] = four
            cols[part, x, pl.ds(4, 4), :] = four

    upper = lax.broadcasted_iota(jnp.int32, (8, CY), 0) < 4
    at_once = min(8, total)

    def send_far(k):
        other = lax.rem(me + k, total)
        return pltpu.make_async_remote_copy(
            src_ref=f_send.at[k],
            dst_ref=f_recv.at[k - 1],
            send_sem=f_send_sem,
            recv_sem=f_recv_sem,
            device_id=(lax.div(other, nx), lax.rem(other, nx)),
            device_id_type=MESH,
        )

    def project(trip, carry):
        k0 = trip * at_once
        picked = [bands[lax.rem(me + k0 + j, total)] for j in range(at_once)]

        def pair(table, part, j):
            return jnp.where(
                upper, table[part, pl.ds(picked[j], 1), :], table[part, pl.ds(picked[j + 1], 1), :]
            )

        pairs = range(0, at_once, 2)
        wr = [pair(cell, 0, j) for j in pairs]
        wi = [pair(cell, 1, j) for j in pairs]
        c_re, c_im = cols[0, CX - 1], cols[1, CX - 1]
        re = [c_re for _ in pairs]
        im = [c_im for _ in pairs]
        for x in range(CX - 2, -1, -1):
            c_re, c_im = cols[0, x], cols[1, x]
            re, im = (
                [r * a - i * b + c_re for r, i, a, b in zip(re, im, wr, wi)],
                [r * b + i * a + c_im for r, i, a, b in zip(re, im, wr, wi)],
            )
        for t, j in enumerate(pairs):
            pr, pi = pair(phase, 0, j), pair(phase, 1, j)
            far_re = re[t] * pr - im[t] * pi
            far_im = re[t] * pi + im[t] * pr
            f_send[k0 + j] = jnp.where(upper, far_re, pltpu.roll(far_im, 4, 0))
            f_send[k0 + j + 1] = jnp.where(upper, pltpu.roll(far_re, 4, 0), far_im)
        for j in range(at_once):
            @pl.when(k0 + j > 0)
            def _(j=j):
                send_far(k0 + j).start()
        return carry

    lax.fori_loop(0, total // at_once, project, 0)

    for c in range(3):
        for z in range(NZ):
            e_out[c, pl.ds(z * CX, CX), :] = ep[c, at(z), :]
            h_out[c, pl.ds(z * CX, CX), :] = hp[c, at(z), :]

    pltpu.make_async_copy(f_recv, f_recv, f_recv_sem).wait()
    if total <= 64:
        terms = [f_send[0]] + [f_recv[k] for k in range(total - 1)]
        while len(terms) > 1:
            terms = [a + b for a, b in zip(terms[::2], terms[1::2])]
        far_out[...] = terms[0]
    else:
        far_out[...] = lax.fori_loop(0, total - 1, lambda k, t: t + f_recv[k], f_send[0])
    pltpu.make_async_copy(f_recv, f_recv, f_send_sem).wait()


def local(ny, nx, electric, magnetic, material_ids, update_ca, update_cb, face_ranges, band_table):
    total = ny * nx
    bands = band_table.shape[0]
    assert bands == total and electric.shape == (3, NZ, CX, CY)
    scale = 1.0 / math.sqrt(CX * nx * CY * ny)
    f32 = jnp.float32
    vmem = pl.BlockSpec(memory_space=pltpu.VMEM)
    smem = pl.BlockSpec(memory_space=pltpu.SMEM)
    rows = NZ * CX
    e_out, h_out, far = pl.pallas_call(
        functools.partial(kernel, ny, nx, scale),
        out_shape=(
            jax.ShapeDtypeStruct((3, rows, CY), f32),
            jax.ShapeDtypeStruct((3, rows, CY), f32),
            jax.ShapeDtypeStruct((8, CY), f32),
        ),
        in_specs=[vmem] * 3 + [smem] * 4 + [vmem] * 5,
        out_specs=(vmem, vmem, vmem),
        scratch_shapes=[
            pltpu.VMEM((3, NZ * PITCH + 8, CY), f32),
            pltpu.VMEM((3, NZ * PITCH + 8, CY), f32),
            pltpu.VMEM((rows, CY), f32),
            pltpu.VMEM((rows, CY), f32),
            pltpu.VMEM((STEPS, 5 * NZ, CY), f32),
            pltpu.VMEM((STEPS, 2 * NZ, CY), f32),
            pltpu.VMEM((STEPS, CX, CY), f32),
            pltpu.VMEM((STEPS, CX, CY), f32),
            pltpu.VMEM((STEPS, 5 * NZ, CY), f32),
            pltpu.VMEM((STEPS, 2 * NZ, CY), f32),
            pltpu.VMEM((STEPS, CX, CY), f32),
            pltpu.VMEM((STEPS, CX, CY), f32),
            pltpu.VMEM((STEPS, NZ, CY), f32),
            pltpu.VMEM((STEPS, 8, CY), f32),
            pltpu.VMEM((4 * CX, CY), f32),
            pltpu.VMEM((2, 4 * CX, CY), f32),
            pltpu.VMEM((2, CX, 8, CY), f32),
            pltpu.VMEM((2, total, CY), f32),
            pltpu.VMEM((total, 8, CY), f32),
            pltpu.VMEM((total - 1, 8, CY), f32),
            pltpu.SemaphoreType.DMA((6,)),
            pltpu.SemaphoreType.DMA((STEPS, 6)),
            pltpu.SemaphoreType.DMA,
            pltpu.SemaphoreType.DMA,
        ],
        compiler_params=pltpu.CompilerParams(
            collective_id=0, has_side_effects=True, vmem_limit_bytes=32 * 1024 * 1024
        ),
        name="fdtd",
    )(
        electric.reshape(3, rows, CY),
        magnetic.reshape(3, rows, CY),
        material_ids.reshape(rows, CY),
        update_ca,
        update_cb,
        face_ranges.reshape(4),
        band_table,
        *tables(bands, ny),
    )
    return (
        e_out.reshape(electric.shape),
        h_out.reshape(electric.shape),
        far.reshape(1, 8, CY),
    )


def solution(mesh):
    in_specs = (
        P(None, None, "inner", "grp"),
        P(None, None, "inner", "grp"),
        P(None, "inner", "grp"),
        P(),
        P(),
        P("inner", "grp", None),
        P(),
    )
    out_specs = (
        P(None, None, "inner", "grp"),
        P(None, None, "inner", "grp"),
        P(("grp", "inner"), None, None),
    )
    body = functools.partial(local, mesh.shape["grp"], mesh.shape["inner"])
    return jax.shard_map(body, mesh=mesh, in_specs=in_specs, out_specs=out_specs, check_vma=False)
```

profile of v0, /device:TPU:0, one launch (start us, length us, event | category | flops | bytes accessed | tf_op | source)
XLA Modules:
  0.0 57.7 jit_solution(9709982325467269263)
XLA Ops:
  0.6 0.0 copy-start.6
  0.6 0.0 copy-start.8
  0.7 0.0 copy-start.9
  0.7 0.7 %copy-done.6 = f32[2,8,128]{2,1,0:T(8,128)S(1)} copy-done((f32[2,8,128]{2,1,0:T(8,128)S(1)}, f32[2,8,128]{2,1,0:T(8,128)}, u32[]{:S(2)}) %copy-start.6) | copy-done | bytes 8216
  1.3 0.0 copy-done.8
  1.3 0.0 copy-done.9
  1.3 0.0 copy-start
  1.3 1.0 %copy-done = f32[3,16,16,128]{3,2,1,0:T(8,128)S(1)} copy-done((f32[3,16,16,128]{3,2,1,0:T(8,128)S(1)}, f32[3,16,16,128]{3,2,1,0:T(8,128)}, u32[]{:S(2)}) %copy-start) | copy-done | bytes 393240
  2.3 0.0 copy-start.1
  2.3 1.0 %copy-done.1 = f32[3,16,16,128]{3,2,1,0:T(8,128)S(1)} copy-done((f32[3,16,16,128]{3,2,1,0:T(8,128)S(1)}, f32[3,16,16,128]{3,2,1,0:T(8,128)}, u32[]{:S(2)}) %copy-start.1) | copy-done | bytes 393240
  3.3 0.0 copy-start.2
  3.3 0.9 %copy-done.2 = s32[16,16,128]{2,1,0:T(8,128)S(1)} copy-done((s32[16,16,128]{2,1,0:T(8,128)S(1)}, s32[16,16,128]{2,1,0:T(8,128)}, u32[]{:S(2)}) %copy-start.2) | copy-done | bytes 131096
  4.2 0.0 copy-start.3
  4.2 0.9 %copy-done.3 = f32[128,256]{1,0:T(8,128)S(1)} copy-done((f32[128,256]{1,0:T(8,128)S(1)}, f32[128,256]{1,0:T(8,128)}, u32[]{:S(2)}) %copy-start.3) | copy-done | bytes 131096
  5.1 0.0 copy-start.4
  5.1 0.8 %copy-done.4 = f32[2,32,128]{2,1,0:T(8,128)S(1)} copy-done((f32[2,32,128]{2,1,0:T(8,128)S(1)}, f32[2,32,128]{2,1,0:T(8,128)}, u32[]{:S(2)}) %copy-start.4) | copy-done | bytes 32792
  5.9 0.0 copy-start.5
  5.9 0.8 %copy-done.5 = f32[2,32,128]{2,1,0:T(8,128)S(1)} copy-done((f32[2,32,128]{2,1,0:T(8,128)S(1)}, f32[2,32,128]{2,1,0:T(8,128)}, u32[]{:S(2)}) %copy-start.5) | copy-done | bytes 32792
  6.7 0.0 copy-start.7
  6.7 0.7 %copy-done.7 = f32[2,4,128]{2,1,0:T(4,128)S(1)} copy-done((f32[2,4,128]{2,1,0:T(4,128)S(1)}, f32[2,4,128]{2,1,0:T(4,128)}, u32[]{:S(2)}) %copy-start.7) | copy-done | bytes 4120
  7.3 0.0 copy-start.10
  7.3 0.7 %copy-done.10 = s32[1,1,4]{2,1,0:T(1,128)S(1)} copy-done((s32[1,1,4]{2,1,0:T(1,128)S(1)}, s32[1,1,4]{2,1,0:T(1,128)}, u32[]{:S(2)}) %copy-start.10) | copy-done | bytes 40
  8.0 0.0 copy-start.11
  8.0 0.7 %copy-done.11 = s32[32]{0:T(128)S(1)} copy-done((s32[32]{0:T(128)S(1)}, s32[32]{0:T(128)}, u32[]{:S(2)}) %copy-start.11) | copy-done | bytes 152
  8.7 47.0 %fdtd.1 = (f32[3,256,128]{2,1,0:T(8,128)S(1)}, f32[3,256,128]{2,1,0:T(8,128)S(1)}, f32[8,128]{1,0:T(8,128)S(1)}) custom-call(f32[3,256,128]{2,1,0:T(8,128)S(1)} %bitcast.7, f32[3,256,128]{2,1,0:T(8,128)S(1)} %bitcast.8, s32[256,128]{1,0:T(8,128)S(1)} %bitcast.11, f32[8]{0:T(128)S(1)} %copy-done.8, f32[8]{0:T(128)S(1)} %copy-done.9, s32[4]{0:T(128)S(1)} %bitcast.13, ...), custom_call_target="tpu_custom_call" | custom-call | tf_op jit(solution)/shard_map/fdtd/pallas_call | solution.py:337
  55.6 0.7 %copy.18 = f32[3,16,16,128]{3,2,1,0:T(8,128)} copy(f32[3,16,16,128]{3,2,1,0:T(8,128)S(1)} %bitcast.10) | data formatting | bytes 786432
  56.4 0.7 %copy.19 = f32[3,16,16,128]{3,2,1,0:T(8,128)} copy(f32[3,16,16,128]{3,2,1,0:T(8,128)S(1)} %bitcast.9) | data formatting | bytes 786432
  57.1 0.6 %copy.20 = f32[1,8,128]{2,1,0:T(8,128)} copy(f32[1,8,128]{2,1,0:T(8,128)S(1)} %bitcast.12) | data formatting | bytes 8192
Async XLA Ops:
  0.6 0.7 %copy-start.6 = (f32[2,8,128]{2,1,0:T(8,128)S(1)}, f32[2,8,128]{2,1,0:T(8,128)}, u32[]{:S(2)}) copy-start(f32[2,8,128]{2,1,0:T(8,128)} %constant.11.clone.time) | copy-start | bytes 24580
  0.6 0.7 %copy-start.8 = (f32[8]{0:T(128)S(1)}, f32[8]{0:T(128)}, u32[]{:S(2)}) copy-start(f32[8]{0:T(128)} %ca.1) | copy-start | bytes 100
  0.7 0.7 %copy-start.9 = (f32[8]{0:T(128)S(1)}, f32[8]{0:T(128)}, u32[]{:S(2)}) copy-start(f32[8]{0:T(128)} %cb.1) | copy-start | bytes 100
  1.3 1.0 %copy-start = (f32[3,16,16,128]{3,2,1,0:T(8,128)S(1)}, f32[3,16,16,128]{3,2,1,0:T(8,128)}, u32[]{:S(2)}) copy-start(f32[3,16,16,128]{3,2,1,0:T(8,128)} %param.12) | copy-start | bytes 1179652
  2.3 1.0 %copy-start.1 = (f32[3,16,16,128]{3,2,1,0:T(8,128)S(1)}, f32[3,16,16,128]{3,2,1,0:T(8,128)}, u32[]{:S(2)}) copy-start(f32[3,16,16,128]{3,2,1,0:T(8,128)} %param.13) | copy-start | bytes 1179652
  3.3 0.9 %copy-start.2 = (s32[16,16,128]{2,1,0:T(8,128)S(1)}, s32[16,16,128]{2,1,0:T(8,128)}, u32[]{:S(2)}) copy-start(s32[16,16,128]{2,1,0:T(8,128)} %param.14) | copy-start | bytes 393220
  4.2 0.9 %copy-start.3 = (f32[128,256]{1,0:T(8,128)S(1)}, f32[128,256]{1,0:T(8,128)}, u32[]{:S(2)}) copy-start(f32[128,256]{1,0:T(8,128)} %constant.10.clone.proj) | copy-start | bytes 393220
  5.1 0.8 %copy-start.4 = (f32[2,32,128]{2,1,0:T(8,128)S(1)}, f32[2,32,128]{2,1,0:T(8,128)}, u32[]{:S(2)}) copy-start(f32[2,32,128]{2,1,0:T(8,128)} %constant.14.clone.block) | copy-start | bytes 98308
  5.9 0.8 %copy-start.5 = (f32[2,32,128]{2,1,0:T(8,128)S(1)}, f32[2,32,128]{2,1,0:T(8,128)}, u32[]{:S(2)}) copy-start(f32[2,32,128]{2,1,0:T(8,128)} %constant.13.clone.cell) | copy-start | bytes 98308
  6.7 0.7 %copy-start.7 = (f32[2,4,128]{2,1,0:T(4,128)S(1)}, f32[2,4,128]{2,1,0:T(4,128)}, u32[]{:S(2)}) copy-start(f32[2,4,128]{2,1,0:T(4,128)} %constant.12.clone.y_start) | copy-start | bytes 12292
  7.3 0.7 %copy-start.10 = (s32[1,1,4]{2,1,0:T(1,128)S(1)}, s32[1,1,4]{2,1,0:T(1,128)}, u32[]{:S(2)}) copy-start(s32[1,1,4]{2,1,0:T(1,128)} %param.17) | copy-start | bytes 52
  8.0 0.7 %copy-start.11 = (s32[32]{0:T(128)S(1)}, s32[32]{0:T(128)}, u32[]{:S(2)}) copy-start(s32[32]{0:T(128)} %bands.1) | copy-start | bytes 388
where the time goes:
time: 58.2 us; the launch traced here: 57.7 us
  Pallas kernels  47 us (81%)
  local copies, waits for them, and re-layouts  10.1 us (17%)
  between operations  0.68 us (1%)
    pallas_call x1, Pallas kernels, local(): pl.pallas_call(functools.partial(kernel, ny, nx, scale), out_shape=(jax.S...  47 us
    unnamed x27, local copies, waits for them, and re-layouts  10.1 us

commit v1 on v0

--- a/solution.py
+++ b/solution.py
@@ -37,13 +37,27 @@
     y_start = np.stack(both(f * b * CY * np.arange(groups, dtype=np.int64)[:, None], 4096))
     cell = np.stack(both(f * a[:, None], 4096))
     block = np.stack(both(f * a[:, None] * CX, 4096))
-    return proj, time, y_start, cell, block
+    flat = [proj[:, :CY], proj[:, CY:]] + [part for table in (time, y_start, cell, block) for part in table]
+    starts = np.cumsum([0] + [-(-part.shape[0] // 8) * 8 for part in flat])
+    packed = np.zeros((starts[-1], CY), np.float32)
+    for start, part in zip(starts, flat):
+        packed[start : start + part.shape[0]] = part
+    return packed, tuple(int(start) for start in starts[:-1])
+
+
+class Rows:
+    def __init__(self, ref, starts):
+        self.ref, self.starts = ref, starts
+
+    def at(self, part, first, count):
+        return self.ref[pl.ds(self.starts[part] + first, count), :]
 
 
 def kernel(
-    ny, nx, scale,
-    e_in, h_in, ids, ca, cb, face, bands, proj, time, y_start, cell, block,
+    ny, nx, scale, starts,
+    e_hbm, h_hbm, ids_hbm, ca_hbm, cb_hbm, face_hbm, bands_hbm, table_hbm,
     e_out, h_out, far_out,
+    e_in, h_in, ids, ca, cb, face, bands, table, in_sem,
     ep, hp, coef_a, coef_b,
     xs_r, xs_l, ys_r, ys_l, xr_l, xr_r, yr_l, yr_r, cor_x, cor_y,
     sample, acc, cols, phase, f_send, f_recv,
@@ -56,6 +70,25 @@
     lane = lax.broadcasted_iota(jnp.int32, (CX, CY), 1)
     row = lax.broadcasted_iota(jnp.int32, (CX, CY), 0)
 
+    loads = [
+        pltpu.make_async_copy(src, dst, in_sem.at[i])
+        for i, (src, dst) in enumerate(
+            (
+                (e_hbm, e_in),
+                (h_hbm, h_in),
+                (ids_hbm, ids),
+                (ca_hbm, ca),
+                (cb_hbm, cb),
+                (face_hbm, face),
+                (bands_hbm, bands),
+                (table_hbm, table),
+            )
+        )
+    ]
+    for load in loads:
+        load.start()
+    time, y_start, cell, block = (Rows(table, starts[i : i + 2]) for i in (2, 4, 6, 8))
+
     for buf in (xr_l, xr_r, yr_l, yr_r, cor_x, cor_y):
         buf[...] = jnp.zeros(buf.shape, jnp.float32)
 
@@ -76,6 +109,8 @@
     def plane(x):
         return pl.ds(BASE + x, NZ, stride=PITCH)
 
+    for load in loads:
+        load.wait()
     for c in range(3):
         for z in range(NZ):
             ep[c, at(z), :] = e_in[c, pl.ds(z * CX, CX), :]
@@ -114,14 +149,15 @@
         carry = (
             jnp.full((rows_at_once, CY), scale, jnp.float32),
             jnp.zeros((rows_at_once, CY), jnp.float32),
-            block[0, part, :],
-            block[1, part, :],
+            block.at(0, start, rows_at_once),
+            block.at(1, start, rows_at_once),
         )
         for bit in range(max(1, (nx - 1).bit_length())):
             carry = power(bit, carry)
-        phase[0, part, :] = carry[0]
-        phase[1, part, :] = carry[1]
-
+        phase[part, :] = carry[0]
+        phase[pl.ds(total + start, rows_at_once), :] = carry[1]
+
+    start_phase = Rows(phase, (0, total))
     pl.semaphore_wait(barrier, total - 1)
 
     has_xr, has_xl = ix < nx - 1, ix > 0
@@ -148,12 +184,16 @@
         )
 
     def add_sample(n):
-        g = jnp.dot(
-            sample[...], proj[...], precision=lax.Precision.HIGHEST, preferred_element_type=jnp.float32
-        )
-        g_re, g_im = g[:, :CY], g[:, CY:]
-        ct = time[0, pl.ds(n, 1), :]
-        st = time[1, pl.ds(n, 1), :]
+        g_re, g_im = (
+            jnp.dot(
+                sample[...],
+                table[pl.ds(starts[part], CY), :],
+                precision=lax.Precision.HIGHEST,
+                preferred_element_type=jnp.float32,
+            )
+            for part in range(2)
+        )
+        ct, st = time.at(0, n, 1), time.at(1, n, 1)
         acc[0] += ct * g_re + st * g_im
         acc[1] += ct * g_im - st * g_re
 
@@ -249,8 +289,7 @@
     lax.fori_loop(0, STEPS, step, 0)
     add_sample(STEPS - 1)
 
-    yr = y_start[0, pl.ds(iy, 1), :]
-    yi = y_start[1, pl.ds(iy, 1), :]
+    yr, yi = y_start.at(0, iy, 1), y_start.at(1, iy, 1)
     col_re = acc[0] * yr - acc[1] * yi
     acc[1] = acc[0] * yi + acc[1] * yr
     acc[0] = col_re
@@ -278,10 +317,8 @@
         k0 = trip * at_once
         picked = [bands[lax.rem(me + k0 + j, total)] for j in range(at_once)]
 
-        def pair(table, part, j):
-            return jnp.where(
-                upper, table[part, pl.ds(picked[j], 1), :], table[part, pl.ds(picked[j + 1], 1), :]
-            )
+        def pair(rows, part, j):
+            return jnp.where(upper, rows.at(part, picked[j], 1), rows.at(part, picked[j + 1], 1))
 
         pairs = range(0, at_once, 2)
         wr = [pair(cell, 0, j) for j in pairs]
@@ -296,7 +333,7 @@
                 [r * b + i * a + c_im for r, i, a, b in zip(re, im, wr, wi)],
             )
         for t, j in enumerate(pairs):
-            pr, pi = pair(phase, 0, j), pair(phase, 1, j)
+            pr, pi = pair(start_phase, 0, j), pair(start_phase, 1, j)
             far_re = re[t] * pr - im[t] * pi
             far_im = re[t] * pi + im[t] * pr
             f_send[k0 + j] = jnp.where(upper, far_re, pltpu.roll(far_im, 4, 0))
@@ -332,18 +369,28 @@
     scale = 1.0 / math.sqrt(CX * nx * CY * ny)
     f32 = jnp.float32
     vmem = pl.BlockSpec(memory_space=pltpu.VMEM)
-    smem = pl.BlockSpec(memory_space=pltpu.SMEM)
+    hbm = pl.BlockSpec(memory_space=pltpu.HBM)
+    packed, starts = tables(bands, ny)
     rows = NZ * CX
     e_out, h_out, far = pl.pallas_call(
-        functools.partial(kernel, ny, nx, scale),
+        functools.partial(kernel, ny, nx, scale, starts),
         out_shape=(
             jax.ShapeDtypeStruct((3, rows, CY), f32),
             jax.ShapeDtypeStruct((3, rows, CY), f32),
             jax.ShapeDtypeStruct((8, CY), f32),
         ),
-        in_specs=[vmem] * 3 + [smem] * 4 + [vmem] * 5,
+        in_specs=[hbm] * 8,
         out_specs=(vmem, vmem, vmem),
         scratch_shapes=[
+            pltpu.VMEM((3, rows, CY), f32),
+            pltpu.VMEM((3, rows, CY), f32),
+            pltpu.VMEM((rows, CY), jnp.int32),
+            pltpu.SMEM((NMAT,), f32),
+            pltpu.SMEM((NMAT,), f32),
+            pltpu.SMEM((4,), jnp.int32),
+            pltpu.SMEM((bands,), jnp.int32),
+            pltpu.VMEM(packed.shape, f32),
+            pltpu.SemaphoreType.DMA((8,)),
             pltpu.VMEM((3, NZ * PITCH + 8, CY), f32),
             pltpu.VMEM((3, NZ * PITCH + 8, CY), f32),
             pltpu.VMEM((rows, CY), f32),
@@ -361,7 +408,7 @@
             pltpu.VMEM((4 * CX, CY), f32),
             pltpu.VMEM((2, 4 * CX, CY), f32),
             pltpu.VMEM((2, CX, 8, CY), f32),
-            pltpu.VMEM((2, total, CY), f32),
+            pltpu.VMEM((2 * total, CY), f32),
             pltpu.VMEM((total, 8, CY), f32),
             pltpu.VMEM((total - 1, 8, CY), f32),
             pltpu.SemaphoreType.DMA((6,)),
@@ -370,7 +417,7 @@
             pltpu.SemaphoreType.DMA,
         ],
         compiler_params=pltpu.CompilerParams(
-            collective_id=0, has_side_effects=True, vmem_limit_bytes=32 * 1024 * 1024
+            collective_id=0, has_side_effects=True, vmem_limit_bytes=62 * 1024 * 1024
         ),
         name="fdtd",
     )(
@@ -381,7 +428,7 @@
         update_cb,
         face_ranges.reshape(4),
         band_table,
-        *tables(bands, ny),
+        packed,
     )
     return (
         e_out.reshape(electric.shape),

time: 58.2 us -> 51.4 us (0.88)
  local copies, waits for them, and re-layouts: 10.1 us -> 3.16 us
    unnamed x27 -> x7, local copies, waits for them, and re-layouts: 10.1 us -> 3.16 us
where the time goes in v1:
time: 51.4 us; the launch traced here: 51.2 us
  Pallas kernels  47.4 us (92%)
  local copies, waits for them, and re-layouts  3.16 us (6%)
  between operations  0.65 us (1%)
    pallas_call x1, Pallas kernels, local(): pl.pallas_call(functools.partial(kernel, ny, nx, scale, starts), out_shap...  47.4 us
    unnamed x7, local copies, waits for them, and re-layouts  3.16 us

profile of v1, /device:TPU:0, one launch (start us, length us, event | category | flops | bytes accessed | tf_op | source)
XLA Modules:
  0.0 51.2 jit_solution(18144226332039911904)
XLA Ops:
  0.6 47.4 %fdtd.1 = (f32[3,256,128]{2,1,0:T(8,128)}, f32[3,256,128]{2,1,0:T(8,128)}, f32[8,128]{1,0:T(8,128)}) custom-call(f32[3,256,128]{2,1,0:T(8,128)} %bitcast.7, f32[3,256,128]{2,1,0:T(8,128)} %bitcast.8, s32[256,128]{1,0:T(8,128)} %bitcast.11, f32[8]{0:T(128)} %ca_hbm.1, f32[8]{0:T(128)} %cb_hbm.1, s32[4]{0:T(128)} %bitcast.13, s32[32]{0:T(128)} %bands_hbm.1, ...), custom_call_target="tpu_custom_call" | custom-call | tf_op jit(solution)/shard_map/fdtd/pallas_call | solution.py:375
  48.0 0.0 copy-start
  48.1 1.8 %copy.14 = f32[3,16,16,128]{3,2,1,0:T(8,128)} copy(f32[3,16,16,128]{3,2,1,0:T(8,128)} %bitcast.10) | data formatting | bytes 786432
  49.9 0.0 copy-done
  49.9 0.0 copy-start.1
  49.9 0.7 %copy.15 = f32[3,16,16,128]{3,2,1,0:T(8,128)} copy(f32[3,16,16,128]{3,2,1,0:T(8,128)S(1)} %bitcast.9) | data formatting | bytes 786432
  50.6 0.0 copy-done.1
  50.6 0.6 %copy.16 = f32[1,8,128]{2,1,0:T(8,128)} copy(f32[1,8,128]{2,1,0:T(8,128)S(1)} %bitcast.12) | data formatting | bytes 8192
Async XLA Ops:
  48.0 1.8 %copy-start = (f32[3,256,128]{2,1,0:T(8,128)S(1)}, f32[3,256,128]{2,1,0:T(8,128)}, u32[]{:S(2)}) copy-start(f32[3,256,128]{2,1,0:T(8,128)} %get-tuple-element.7) | copy-start | bytes 1179652
  49.9 0.8 %copy-start.1 = (f32[8,128]{1,0:T(8,128)S(1)}, f32[8,128]{1,0:T(8,128)}, u32[]{:S(2)}) copy-start(f32[8,128]{1,0:T(8,128)} %get-tuple-element.8) | copy-start | bytes 12292

commit v2 on v1

--- a/solution.py
+++ b/solution.py
@@ -61,7 +61,7 @@
     ep, hp, coef_a, coef_b,
     xs_r, xs_l, ys_r, ys_l, xr_l, xr_r, yr_l, yr_r, cor_x, cor_y,
     sample, acc, cols, phase, f_send, f_recv,
-    send_sem, recv_sem, f_send_sem, f_recv_sem,
+    send_sem, recv_sem, f_send_sem, f_recv_sem, hx_send, hx_recv, once_sem,
 ):
     iy = lax.axis_index("grp")
     ix = lax.axis_index("inner")
@@ -89,7 +89,7 @@
         load.start()
     time, y_start, cell, block = (Rows(table, starts[i : i + 2]) for i in (2, 4, 6, 8))
 
-    for buf in (xr_l, xr_r, yr_l, yr_r, cor_x, cor_y):
+    for buf in (hx_recv, xr_l, xr_r, yr_l, yr_r, cor_x, cor_y):
         buf[...] = jnp.zeros(buf.shape, jnp.float32)
 
     barrier = pltpu.get_barrier_semaphore()
@@ -109,6 +109,8 @@
     def plane(x):
         return pl.ds(BASE + x, NZ, stride=PITCH)
 
+    for c in (1, 2):
+        ep[c, plane(CX), :] = jnp.zeros((NZ, CY), jnp.float32)
     for load in loads:
         load.wait()
     for c in range(3):
@@ -183,6 +185,15 @@
             device_id_type=MESH,
         )
 
+    def start_copies(n, which):
+        every = copies(n)
+        for i in which:
+            sends, _, src, dst, device = every[i]
+
+            @pl.when(sends)
+            def _(i=i, src=src, dst=dst, device=device):
+                remote(n, i, src, dst, device).start()
+
     def add_sample(n):
         g_re, g_im = (
             jnp.dot(
@@ -200,10 +211,11 @@
     def step(n, carry):
         last = jnp.zeros((CX, CY), jnp.float32)
         first = jnp.zeros((CX, CY), jnp.float32)
-        for g, (field, c) in enumerate(((ep, 0), (ep, 1), (ep, 2), (hp, 1), (hp, 2))):
-            xs_r[n, pl.ds(g * NZ, NZ), :] = field[c, plane(CX - 1), :]
+        for c in range(3):
+            xs_r[n, pl.ds(c * NZ, NZ), :] = ep[c, plane(CX - 1), :]
         for g, c in enumerate((1, 2)):
             xs_l[n, pl.ds(g * NZ, NZ), :] = ep[c, plane(0), :]
+        start_copies(n, (4, 0, 1))
         for z in range(NZ):
             for g, (field, c) in enumerate(((ep, 0), (ep, 1), (ep, 2), (hp, 0), (hp, 2))):
                 spot = g * NZ + z
@@ -214,11 +226,20 @@
                 first = jnp.where(lane == spot, pltpu.roll(value, spot, 1) if spot else value, first)
         ys_r[n] = last
         ys_l[n] = first
-        for i, (sends, _, src, dst, device) in enumerate(copies(n)):
-            @pl.when(sends)
-            def _(i=i, src=src, dst=dst, device=device):
-                remote(n, i, src, dst, device).start()
-
+        start_copies(n, (5, 2, 3))
+
+        zero = jnp.zeros((CX, CY), jnp.float32)
+        for z in range(NZ):
+            ex, ey, ez = (ep[c, at(z), :] for c in range(3))
+            ex_z = ep[0, at(z + 1), :] if z < NZ - 1 else zero
+            ey_z = ep[1, at(z + 1), :] if z < NZ - 1 else zero
+            ey_x = ep[1, at(z, 1), :]
+            ez_x = ep[2, at(z, 1), :]
+            ex_y = jnp.where(lane == CY - 1, 0.0, pltpu.roll(ex, CY - 1, 1))
+            ez_y = jnp.where(lane == CY - 1, 0.0, pltpu.roll(ez, CY - 1, 1))
+            hp[0, at(z), :] = hp[0, at(z), :] - 0.5 * ((ez_y - ez) - (ey_z - ey))
+            hp[1, at(z), :] = hp[1, at(z), :] - 0.5 * ((ex_z - ex) - (ez_x - ez))
+            hp[2, at(z), :] = hp[2, at(z), :] - 0.5 * ((ey_x - ey) - (ex_y - ex))
         add_sample(jnp.maximum(n - 1, 0))
 
         for i, (_, receives, src, dst, _) in enumerate(copies(n)):
@@ -226,10 +247,20 @@
             def _(i=i, src=src, dst=dst):
                 remote(n, i, src, dst, (iy, ix)).wait_recv()
 
-        ex, ey, ez, hy, hz = (xr_l[n, pl.ds(g * NZ, NZ), :] for g in range(5))
+        @pl.when(n == 0)
+        def _():
+            @pl.when(has_xl)
+            def _():
+                once.wait_recv()
+
+            for g, c in enumerate((1, 2)):
+                hp[c, plane(-1), :] = hx_recv[pl.ds(g * NZ, NZ), :]
+
+        ex, ey, ez = (xr_l[n, pl.ds(g * NZ, NZ), :] for g in range(3))
+        hy, hz = hp[1, plane(-1), :], hp[2, plane(-1), :]
         ey0, ez0 = xs_l[n, pl.ds(0, NZ), :], xs_l[n, pl.ds(NZ, NZ), :]
-        ep[1, plane(CX), :] = xr_r[n, pl.ds(0, NZ), :]
-        ep[2, plane(CX), :] = xr_r[n, pl.ds(NZ, NZ), :]
+        hp[1, plane(CX - 1), :] += 0.5 * xr_r[n, pl.ds(NZ, NZ), :]
+        hp[2, plane(CX - 1), :] -= 0.5 * xr_r[n, pl.ds(0, NZ), :]
         ex_z = jnp.where(row == NZ - 1, 0.0, pltpu.roll(ex, NZ - 1, 0))
         ex_y = pltpu.roll(jnp.where(lane == 0, cor_x[n], ex), CY - 1, 1)
         hp[1, plane(-1), :] = inside_x * (hy - 0.5 * ((ex_z - ex) - (ez0 - ez)))
@@ -245,25 +276,13 @@
         hx_col = inside_y * (hx - 0.5 * ((ez0 - ez) - (ey_z - ey)))
         hz_col = inside_y * (hz - 0.5 * ((ey_x - ey) - (ex0 - ex)))
 
-        after = yr_r[n]
-        zero = jnp.zeros((CX, CY), jnp.float32)
+        after = 0.5 * yr_r[n]
         for z in range(NZ):
-            ex, ey, ez = (ep[c, at(z), :] for c in range(3))
-            ex_z = ep[0, at(z + 1), :] if z < NZ - 1 else zero
-            ey_z = ep[1, at(z + 1), :] if z < NZ - 1 else zero
-            ey_x = ep[1, at(z, 1), :]
-            ez_x = ep[2, at(z, 1), :]
-            ex_y = jnp.where(
-                lane == CY - 1, pltpu.roll(after, CY - 1 - z, 1), pltpu.roll(ex, CY - 1, 1)
-            )
-            ez_y = jnp.where(
-                lane == CY - 1, pltpu.roll(after, CY - 1 - NZ - z, 1), pltpu.roll(ez, CY - 1, 1)
-            )
-            hp[0, at(z), :] = hp[0, at(z), :] - 0.5 * ((ez_y - ez) - (ey_z - ey))
-            hp[1, at(z), :] = hp[1, at(z), :] - 0.5 * ((ex_z - ex) - (ez_x - ez))
-            hp[2, at(z), :] = hp[2, at(z), :] - 0.5 * ((ey_x - ey) - (ex_y - ex))
-        for z in range(NZ):
-            hx, hy, hz = (hp[c, at(z), :] for c in range(3))
+            hy = hp[1, at(z), :]
+            hx = hp[0, at(z), :] - jnp.where(lane == CY - 1, pltpu.roll(after, CY - 1 - NZ - z, 1), 0.0)
+            hz = hp[2, at(z), :] + jnp.where(lane == CY - 1, pltpu.roll(after, CY - 1 - z, 1), 0.0)
+            hp[0, at(z), :] = hx
+            hp[2, at(z), :] = hz
             hx_z = hp[0, at(z - 1), :] if z else zero
             hy_z = hp[1, at(z - 1), :] if z else zero
             hy_x = hp[1, at(z, -1), :]
@@ -286,7 +305,27 @@
                 remote(n, i, src, dst, device).wait_send()
         return carry
 
+    once = pltpu.make_async_remote_copy(
+        src_ref=hx_send,
+        dst_ref=hx_recv,
+        send_sem=once_sem.at[0],
+        recv_sem=once_sem.at[1],
+        device_id=(iy, ix + 1),
+        device_id_type=MESH,
+    )
+    for g, c in enumerate((1, 2)):
+        hx_send[pl.ds(g * NZ, NZ), :] = hp[c, plane(CX - 1), :]
+
+    @pl.when(has_xr)
+    def _():
+        once.start()
+
     lax.fori_loop(0, STEPS, step, 0)
+
+    @pl.when(has_xr)
+    def _():
+        once.wait_send()
+
     add_sample(STEPS - 1)
 
     yr, yi = y_start.at(0, iy, 1), y_start.at(1, iy, 1)
@@ -395,11 +434,11 @@
             pltpu.VMEM((3, NZ * PITCH + 8, CY), f32),
             pltpu.VMEM((rows, CY), f32),
             pltpu.VMEM((rows, CY), f32),
-            pltpu.VMEM((STEPS, 5 * NZ, CY), f32),
+            pltpu.VMEM((STEPS, 3 * NZ, CY), f32),
             pltpu.VMEM((STEPS, 2 * NZ, CY), f32),
             pltpu.VMEM((STEPS, CX, CY), f32),
             pltpu.VMEM((STEPS, CX, CY), f32),
-            pltpu.VMEM((STEPS, 5 * NZ, CY), f32),
+            pltpu.VMEM((STEPS, 3 * NZ, CY), f32),
             pltpu.VMEM((STEPS, 2 * NZ, CY), f32),
             pltpu.VMEM((STEPS, CX, CY), f32),
             pltpu.VMEM((STEPS, CX, CY), f32),
@@ -415,6 +454,9 @@
             pltpu.SemaphoreType.DMA((STEPS, 6)),
             pltpu.SemaphoreType.DMA,
             pltpu.SemaphoreType.DMA,
+            pltpu.VMEM((2 * NZ, CY), f32),
+            pltpu.VMEM((2 * NZ, CY), f32),
+            pltpu.SemaphoreType.DMA((2,)),
         ],
         compiler_params=pltpu.CompilerParams(
             collective_id=0, has_side_effects=True, vmem_limit_bytes=62 * 1024 * 1024

time: 51.4 us -> 49.7 us (0.967)
  Pallas kernels: 47.4 us -> 45.8 us
    pallas_call x1, Pallas kernels: 47.4 us -> 45.8 us  [local(): pl.pallas_call(functools.partial(kernel, ny, nx, scale, starts), out_shap...]
where the time goes in v2:
time: 49.7 us; the launch traced here: 49.6 us
  Pallas kernels  45.8 us (92%)
  local copies, waits for them, and re-layouts  3.16 us (6%)
  between operations  0.65 us (1%)
    pallas_call x1, Pallas kernels, local(): pl.pallas_call(functools.partial(kernel, ny, nx, scale, starts), out_shap...  45.8 us
    unnamed x7, local copies, waits for them, and re-layouts  3.16 us

profile of v2, /device:TPU:0, one launch (start us, length us, event | category | flops | bytes accessed | tf_op | source)
XLA Modules:
  0.0 49.6 jit_solution(5922673902874965263)
XLA Ops:
  0.6 45.8 %fdtd.1 = (f32[3,256,128]{2,1,0:T(8,128)}, f32[3,256,128]{2,1,0:T(8,128)}, f32[8,128]{1,0:T(8,128)}) custom-call(f32[3,256,128]{2,1,0:T(8,128)} %bitcast.7, f32[3,256,128]{2,1,0:T(8,128)} %bitcast.8, s32[256,128]{1,0:T(8,128)} %bitcast.11, f32[8]{0:T(128)} %ca_hbm.1, f32[8]{0:T(128)} %cb_hbm.1, s32[4]{0:T(128)} %bitcast.13, s32[32]{0:T(128)} %bands_hbm.1, ...), custom_call_target="tpu_custom_call" | custom-call | tf_op jit(solution)/shard_map/fdtd/pallas_call | solution.py:414
  46.4 0.0 copy-start
  46.4 1.8 %copy.14 = f32[3,16,16,128]{3,2,1,0:T(8,128)} copy(f32[3,16,16,128]{3,2,1,0:T(8,128)} %bitcast.10) | data formatting | bytes 786432
  48.2 0.0 copy-done
  48.2 0.0 copy-start.1
  48.2 0.7 %copy.15 = f32[3,16,16,128]{3,2,1,0:T(8,128)} copy(f32[3,16,16,128]{3,2,1,0:T(8,128)S(1)} %bitcast.9) | data formatting | bytes 786432
  49.0 0.0 copy-done.1
  49.0 0.6 %copy.16 = f32[1,8,128]{2,1,0:T(8,128)} copy(f32[1,8,128]{2,1,0:T(8,128)S(1)} %bitcast.12) | data formatting | bytes 8192
Async XLA Ops:
  46.4 1.8 %copy-start = (f32[3,256,128]{2,1,0:T(8,128)S(1)}, f32[3,256,128]{2,1,0:T(8,128)}, u32[]{:S(2)}) copy-start(f32[3,256,128]{2,1,0:T(8,128)} %get-tuple-element.7) | copy-start | bytes 1179652
  48.2 0.8 %copy-start.1 = (f32[8,128]{1,0:T(8,128)S(1)}, f32[8,128]{1,0:T(8,128)}, u32[]{:S(2)}) copy-start(f32[8,128]{1,0:T(8,128)} %get-tuple-element.8) | copy-start | bytes 12292

commit v3 on v2

--- a/solution.py
+++ b/solution.py
@@ -215,7 +215,7 @@
             xs_r[n, pl.ds(c * NZ, NZ), :] = ep[c, plane(CX - 1), :]
         for g, c in enumerate((1, 2)):
             xs_l[n, pl.ds(g * NZ, NZ), :] = ep[c, plane(0), :]
-        start_copies(n, (4, 0, 1))
+        start_copies(n, (0, 1, 4))
         for z in range(NZ):
             for g, (field, c) in enumerate(((ep, 0), (ep, 1), (ep, 2), (hp, 0), (hp, 2))):
                 spot = g * NZ + z

time: 49.7 us -> 50 us (level)
  no operation moved by 1% of the time
where the time goes in v3:
time: 50 us; the launch traced here: 49.9 us
  Pallas kernels  46.1 us (92%)
  local copies, waits for them, and re-layouts  3.16 us (6%)
  between operations  0.65 us (1%)
    pallas_call x1, Pallas kernels, local(): pl.pallas_call(functools.partial(kernel, ny, nx, scale, starts), out_shap...  46.1 us
    unnamed x7, local copies, waits for them, and re-layouts  3.16 us

profile of v3, /device:TPU:0, one launch (start us, length us, event | category | flops | bytes accessed | tf_op | source)
XLA Modules:
  0.0 49.9 jit_solution(16596229416368117514)
XLA Ops:
  0.6 46.1 %fdtd.1 = (f32[3,256,128]{2,1,0:T(8,128)}, f32[3,256,128]{2,1,0:T(8,128)}, f32[8,128]{1,0:T(8,128)}) custom-call(f32[3,256,128]{2,1,0:T(8,128)} %bitcast.7, f32[3,256,128]{2,1,0:T(8,128)} %bitcast.8, s32[256,128]{1,0:T(8,128)} %bitcast.11, f32[8]{0:T(128)} %ca_hbm.1, f32[8]{0:T(128)} %cb_hbm.1, s32[4]{0:T(128)} %bitcast.13, s32[32]{0:T(128)} %bands_hbm.1, ...), custom_call_target="tpu_custom_call" | custom-call | tf_op jit(solution)/shard_map/fdtd/pallas_call | solution.py:414
  46.7 0.0 copy-start
  46.7 1.8 %copy.14 = f32[3,16,16,128]{3,2,1,0:T(8,128)} copy(f32[3,16,16,128]{3,2,1,0:T(8,128)} %bitcast.10) | data formatting | bytes 786432
  48.5 0.0 copy-done
  48.5 0.0 copy-start.1
  48.5 0.7 %copy.15 = f32[3,16,16,128]{3,2,1,0:T(8,128)} copy(f32[3,16,16,128]{3,2,1,0:T(8,128)S(1)} %bitcast.9) | data formatting | bytes 786432
  49.3 0.0 copy-done.1
  49.3 0.6 %copy.16 = f32[1,8,128]{2,1,0:T(8,128)} copy(f32[1,8,128]{2,1,0:T(8,128)S(1)} %bitcast.12) | data formatting | bytes 8192
Async XLA Ops:
  46.7 1.8 %copy-start = (f32[3,256,128]{2,1,0:T(8,128)S(1)}, f32[3,256,128]{2,1,0:T(8,128)}, u32[]{:S(2)}) copy-start(f32[3,256,128]{2,1,0:T(8,128)} %get-tuple-element.7) | copy-start | bytes 1179652
  48.5 0.8 %copy-start.1 = (f32[8,128]{1,0:T(8,128)S(1)}, f32[8,128]{1,0:T(8,128)}, u32[]{:S(2)}) copy-start(f32[8,128]{1,0:T(8,128)} %get-tuple-element.8) | copy-start | bytes 12292
